TPU v7x, 32 devices: a whole 2x2x4 slice. The times are simulated.
32 devices in a mesh: dev: 32 (over z, y, x, core).
Axes of the slice: x: 2, y: 2, z: 4, core: 2. Of those that a mesh axis runs over, the one named last changes fastest.
Arguments:
- saved: bfloat16 [32, 1024, 768], P('dev'), may hold values from -6 to 6
- cotangent: bfloat16 [32, 1024, 2048], P('dev'), may hold values from -6 to 6
- weights: bfloat16 [32, 768, 2048], P('dev'), may hold values from -0.21875 to 0.21875
- counts: int32 [16], replicated, may hold values from 1 to 8, as said below
- live_rows: int32 [32], P('dev'), may hold values from 1 to 1024, 20480 in all
- next_map: int32 [32], replicated, may hold values from 0 to 15, as said below
- master: float32 [16, 768, 2048], P(None, 'dev'), may hold values from -0.21875 to 0.21875
- moment1: bfloat16 [16, 768, 2048], P(None, 'dev'), may hold values from -6 to 6
- moment2: bfloat16 [16, 768, 2048], P(None, 'dev'), may hold values from 0.049804688 to 4
Outputs:
- input_grads: bfloat16 [32, 1024, 768], P('dev')
- master_out: float32 [16, 768, 2048], P(None, 'dev')
- moment1_out: bfloat16 [16, 768, 2048], P(None, 'dev')
- moment2_out: bfloat16 [16, 768, 2048], P(None, 'dev')
- next_weights: bfloat16 [32, 768, 2048], P('dev')
Inputs may be any that keep to these rules, and one draw needn't show every extreme that they name: The counts sum to 32; in the current placement expert e holds the counts[e] slots that follow those of experts below e; some expert has exactly 8 replicas. `next_map`: every expert is named by 1 to 8 slots; some expert by exactly 8. `live_rows`: the live rows of all slots sum to 20480, and some slot has exactly 1024.
All inputs are finite; a program needn't handle non-finite values. No bound on the sum of `live_rows` on one device may be relied on, other than what follows from the above.
Results may differ from a plain program's by a relative error of at most 0.0058.
Values may be sent and summed in bfloat16 or wider, within the bound.
A program may use at most 128 MiB of HBM per device.

v0:
```python
import jax
import jax.numpy as jnp
from jax import lax
from jax.sharding import PartitionSpec as P

LEARN_RATE = 0.001
DECAY_RATE = 0.1
BETA_ONE = 0.9
BETA_TWO = 0.95
BIAS_ONE = 1.0 - 0.9**20
BIAS_TWO = 1.0 - 0.95**20
EPSILON = 1e-08


def contract_rows(left, right):
    return lax.dot_general(
        left, right, (((0,), (0,)), ((), ())), preferred_element_type=jnp.float32
    )


def contract_cols(left, right):
    return lax.dot_general(
        left, right, (((1,), (1,)), ((), ())), preferred_element_type=jnp.float32
    )


def per_device(saved, cotangent, weights, counts, live_rows, next_map, master, moment1, moment2):
    hidden_rows = saved[0]
    cot_rows = cotangent[0]
    slot_weights = weights[0]
    live_count = live_rows[0]
    row_count = hidden_rows.shape[0]
    devices = lax.axis_size("dev")
    expert_count, share_rows, model_width = master.shape
    row_index = jnp.arange(row_count, dtype=jnp.int32)
    masked = jnp.where((row_index < live_count)[:, None], cot_rows, jnp.zeros_like(cot_rows))
    input_grads = contract_cols(masked, slot_weights).astype(jnp.bfloat16)
    weight_sum = contract_rows(hidden_rows, masked)
    slot_grads = weight_sum.astype(jnp.bfloat16)
    slot_index = jnp.arange(devices, dtype=jnp.int32)
    bounds = jnp.cumsum(counts)
    holders = jnp.sum((bounds[None, :] <= slot_index[:, None]).astype(jnp.int32), axis=1)
    selector = (jnp.arange(expert_count, dtype=jnp.int32)[:, None] == holders[None, :]).astype(
        jnp.bfloat16
    )
    received = lax.all_to_all(slot_grads, "dev", split_axis=0, concat_axis=0, tiled=True)
    columns = received.shape[1]
    pieces = received.reshape(devices, share_rows, columns)
    expert_grads = jnp.einsum("es,src->erc", selector, pieces, preferred_element_type=jnp.float32)
    first_moment = BETA_ONE * moment1.astype(jnp.float32) + (1.0 - BETA_ONE) * expert_grads
    second_moment = (
        BETA_TWO * moment2.astype(jnp.float32) + (1.0 - BETA_TWO) * expert_grads * expert_grads
    )
    update = (
        first_moment / BIAS_ONE / (jnp.sqrt(second_moment / BIAS_TWO) + EPSILON)
        + DECAY_RATE * master
    )
    master_out = master - LEARN_RATE * update
    outgoing = jnp.take(master_out.astype(jnp.bfloat16), next_map, axis=0).reshape(
        devices * share_rows, model_width
    )
    arriving = lax.all_to_all(outgoing, "dev", split_axis=0, concat_axis=0, tiled=True)
    return (
        input_grads[None],
        master_out,
        first_moment.astype(jnp.bfloat16),
        second_moment.astype(jnp.bfloat16),
        arriving[None],
    )


def solution(mesh):
    placed = (
        P("dev", None, None),
        P("dev", None, None),
        P("dev", None, None),
        P(),
        P("dev"),
        P(),
        P(None, "dev", None),
        P(None, "dev", None),
        P(None, "dev", None),
    )
    return jax.shard_map(
        per_device,
        mesh=mesh,
        in_specs=placed,
        out_specs=(
            P("dev", None, None),
            P(None, "dev", None),
            P(None, "dev", None),
            P(None, "dev", None),
            P("dev", None, None),
        ),
        check_vma=False,
    )
```

profile of v0, /device:TPU:0, one launch (start us, length us, event | category | flops | bytes accessed | tf_op | source)
XLA Modules:
  0.0 196.4 jit_solution(3282633967773543695)
XLA Ops:
  0.6 0.0 copy-start
  1.5 8.0 %fusion.4 = bf16[2048,768]{0,1:T(8,128)(2,1)} fusion(bf16[1,1024,2048]{2,1,0:T(8,128)(2,1)} %param.10, pred[1024]{0:T(1024)(128)(4,1)S(1)} %iota_compare_fusion.2, bf16[1,1024,768]{2,1,0:T(8,128)(2,1)} %param.9), kind=kOutput, calls=%fused_computation.7 | convolution fusion | flops 3224895488 | bytes 8913920 | tf_op jit(solution)/shard_map/dot_general | solution.py:16
  9.5 0.0 copy-start.4
  9.5 0.0 copy-start.5
  9.5 7.6 %all-to-all-start = ((bf16[32,24,2048]{2,1,0:T(8,128)(2,1)}), bf16[32,24,2048]{2,1,0:T(8,128)(2,1)}, u32[]{:S(2)}, u32[]{:S(2)}) async-start(bf16[32,24,2048]{2,1,0:T(8,128)(2,1)} %bitcast.35), calls=%async_computation | async-start | bytes 6291456 | tf_op jit(solution)/shard_map/all_to_all | solution.py:46
  17.1 0.0 copy-done.4
  17.1 0.1 copy.44
  17.2 0.1 reduce
  17.4 0.0 copy-done.5
  17.4 0.1 convert_reduce_fusion
  17.5 71.0 %all-to-all-done = bf16[32,24,2048]{2,1,0:T(8,128)(2,1)} async-done(((bf16[32,24,2048]{2,1,0:T(8,128)(2,1)}), bf16[32,24,2048]{2,1,0:T(8,128)(2,1)}, u32[]{:S(2)}, u32[]{:S(2)}) %all-to-all-start) | async-done | bytes 3145760 | tf_op jit(solution)/shard_map/all_to_all | solution.py:46
  88.4 18.7 %fusion.29 = (bf16[16,24,2048]{2,0,1:T(8,128)(2,1)S(1)}, f32[16,24,2048]{2,0,1:T(8,128)}, bf16[16,24,2048]{2,0,1:T(8,128)(2,1)}, bf16[16,24,2048]{2,0,1:T(8,128)(2,1)}) fusion(bf16[16,24,2048]{2,1,0:T(8,128)(2,1)} %param.17, bf16[16,24,2048]{2,1,0:T(8,128)(2,1)} %param.16, f32[16,24,2048]{2,1,0:T(8,128)} %param.15, bf16[32,24,2048]{2,1,0:T(8,128)(2,1)} %all-to-all-done, ...), kind=kOutput, calls=%fused_computation.31 | convolution fusion | flops 66060800 | bytes 17301632 | tf_op jit(solution)/shard_map/es,src->erc/dot_general | solution.py:49
  107.1 2.0 %copy.49 = bf16[16,24,2048]{2,1,0:T(8,128)(2,1)} copy(bf16[16,24,2048]{2,0,1:T(8,128)(2,1)S(1)} %get-tuple-element.25) | data formatting | bytes 3145728 | tf_op jit(solution)/shard_map/convert_element_type | solution.py:59
  109.1 3.8 %gather_fusion = bf16[32,24,2048]{2,1,0:T(8,128)(2,1)} fusion(bf16[16,24,2048]{2,1,0:T(8,128)(2,1)} %copy.49, s32[1024]{0:T(1024)S(1)} %pad_clamp_fusion), kind=kCustom, calls=%fused_computation | custom fusion | bytes 6291584 | tf_op jit(solution)/shard_map/jit(_take)/gather | solution.py:59
  113.0 3.9 %broadcast_select_fusion.1 = bf16[32,24,2048]{2,1,0:T(8,128)(2,1)} fusion(bf16[32,24,2048]{2,1,0:T(8,128)(2,1)} %gather_fusion, pred[32]{0:T(512)(128)(4,1)S(1)} %compare_and_fusion), kind=kLoop, calls=%fused_computation.14 | loop fusion | flops 1572864 | bytes 6291488 | tf_op jit(solution)/shard_map/jit(_take)/select_n | solution.py:59
  116.9 4.2 %all-to-all-start.1 = ((bf16[32,24,2048]{2,1,0:T(8,128)(2,1)}), bf16[32,24,2048]{2,1,0:T(8,128)(2,1)}, u32[]{:S(2)}, u32[]{:S(2)}) async-start(bf16[32,24,2048]{2,1,0:T(8,128)(2,1)} %broadcast_select_fusion.1), calls=%async_computation.1 | async-start | bytes 6291456 | tf_op jit(solution)/shard_map/all_to_all | solution.py:62
  121.1 0.0 copy-done
  121.1 0.0 copy-start.1
  121.1 6.9 %fusion.19 = bf16[1,1024,768]{2,1,0:T(8,128)(2,1)} fusion(bf16[1,768,2048]{2,1,0:T(8,128)(2,1)S(1)} %copy-done, bf16[1,1024,2048]{2,1,0:T(8,128)(2,1)} %param.10, pred[1024]{0:T(1024)(128)(4,1)S(1)} %iota_compare_fusion.2), kind=kOutput, calls=%fused_computation.19 | convolution fusion | flops 3224109056 | bytes 8913920 | tf_op jit(solution)/shard_map/dot_general | solution.py:22
  128.1 0.0 copy-done.1
  128.1 0.0 copy-start.3
  128.1 3.5 %copy.50 = f32[16,24,2048]{2,1,0:T(8,128)} copy(f32[16,24,2048]{2,0,1:T(8,128)S(1)} %copy-done.1) | data formatting | bytes 6291456
  131.6 0.0 copy-start.2
  131.6 0.0 copy-done.3
  131.6 2.0 %copy.51 = bf16[16,24,2048]{2,1,0:T(8,128)(2,1)} copy(bf16[16,24,2048]{2,0,1:T(8,128)(2,1)S(1)} %copy-done.3) | data formatting | bytes 3145728
  133.6 0.0 copy-done.2
  133.6 2.0 %copy.52 = bf16[16,24,2048]{2,1,0:T(8,128)(2,1)} copy(bf16[16,24,2048]{2,0,1:T(8,128)(2,1)S(1)} %copy-done.2) | data formatting | bytes 3145728
  135.6 56.8 %all-to-all-done.1 = bf16[32,24,2048]{2,1,0:T(8,128)(2,1)} async-done(((bf16[32,24,2048]{2,1,0:T(8,128)(2,1)}), bf16[32,24,2048]{2,1,0:T(8,128)(2,1)}, u32[]{:S(2)}, u32[]{:S(2)}) %all-to-all-start.1) | async-done | bytes 3145760 | tf_op jit(solution)/shard_map/all_to_all | solution.py:62
  192.4 4.0 %copy.67 = bf16[1,768,2048]{2,1,0:T(8,128)(2,1)} copy(bf16[1,768,2048]{2,1,0:T(8,128)(2,1)} %bitcast.9) | data formatting | bytes 6291456
  (5 shorter events, 0.1 us)
Async XLA Ops:
  0.6 120.5 %copy-start = (bf16[1,768,2048]{2,1,0:T(8,128)(2,1)S(1)}, bf16[1,768,2048]{2,1,0:T(8,128)(2,1)}, u32[]{:S(2)}) copy-start(bf16[1,768,2048]{2,1,0:T(8,128)(2,1)} %param.11) | copy-start | bytes 9437188
  9.5 7.6 %copy-start.4 = (s32[16]{0:T(128)S(1)}, s32[16]{0:T(128)}, u32[]{:S(2)}) copy-start(s32[16]{0:T(128)} %param.12) | copy-start | bytes 196
  9.5 7.9 %copy-start.5 = (s32[32]{0:T(128)S(1)}, s32[32]{0:T(128)}, u32[]{:S(2)}) copy-start(s32[32]{0:T(128)} %param.14) | copy-start | bytes 388
  9.5 78.9 %all-to-all-start = ((bf16[32,24,2048]{2,1,0:T(8,128)(2,1)}), bf16[32,24,2048]{2,1,0:T(8,128)(2,1)}, u32[]{:S(2)}, u32[]{:S(2)}) async-start(bf16[32,24,2048]{2,1,0:T(8,128)(2,1)} %bitcast.35), calls=%async_computation | async-start | bytes 6291456 | tf_op jit(solution)/shard_map/all_to_all | solution.py:46
  116.9 75.5 %all-to-all-start.1 = ((bf16[32,24,2048]{2,1,0:T(8,128)(2,1)}), bf16[32,24,2048]{2,1,0:T(8,128)(2,1)}, u32[]{:S(2)}, u32[]{:S(2)}) async-start(bf16[32,24,2048]{2,1,0:T(8,128)(2,1)} %broadcast_select_fusion.1), calls=%async_computation.1 | async-start | bytes 6291456 | tf_op jit(solution)/shard_map/all_to_all | solution.py:62
  121.1 7.0 %copy-start.1 = (f32[16,24,2048]{2,0,1:T(8,128)S(1)}, f32[16,24,2048]{2,0,1:T(8,128)}, u32[]{:S(2)}) copy-start(f32[16,24,2048]{2,0,1:T(8,128)} %get-tuple-element.26) | copy-start | bytes 9437188
  128.1 3.5 %copy-start.3 = (bf16[16,24,2048]{2,0,1:T(8,128)(2,1)S(1)}, bf16[16,24,2048]{2,0,1:T(8,128)(2,1)}, u32[]{:S(2)}) copy-start(bf16[16,24,2048]{2,0,1:T(8,128)(2,1)} %get-tuple-element.28) | copy-start | bytes 4718596
  131.6 2.0 %copy-start.2 = (bf16[16,24,2048]{2,0,1:T(8,128)(2,1)S(1)}, bf16[16,24,2048]{2,0,1:T(8,128)(2,1)}, u32[]{:S(2)}) copy-start(bf16[16,24,2048]{2,0,1:T(8,128)(2,1)} %get-tuple-element.27) | copy-start | bytes 4718596
where the time goes:
time: 197 us; the launch traced here: 196 us
  waiting for transfers between devices  128 us (65%)
  matrix products  33.7 us (17%)
  local copies, waits for them, and re-layouts  17.4 us (9%)
  starting transfers between devices  11.8 us (6%)
  other arithmetic  4.2 us (2%)
    all_to_all x1, waiting for transfers between devices, per_device(): lax.all_to_all(slot_grads, 'dev', split_axis=0, concat_axis=0, tiled=True)  71 us
    all_to_all x1, waiting for transfers between devices, per_device(): lax.all_to_all(outgoing, 'dev', split_axis=0, concat_axis=0, tiled=True)  56.8 us
    dot_general x1, matrix products, per_device(): jnp.einsum('es,src->erc', selector, pieces, preferred_element_type=jnp.fl...  18.7 us
    unnamed x16, local copies, waits for them, and re-layouts  11.5 us
    dot_general x1, matrix products, contract_rows(): lax.dot_general(left, right, (((0,), (0,)), ((), ())), preferred_element_...  8.04 us
    all_to_all x1, starting transfers between devices, per_device(): lax.all_to_all(slot_grads, 'dev', split_axis=0, concat_axis=0, tiled=True)  7.59 us
    dot_general x1, matrix products, contract_cols(): lax.dot_general(left, right, (((1,), (1,)), ((), ())), preferred_element_...  6.95 us
    all_to_all x1, starting transfers between devices, per_device(): lax.all_to_all(outgoing, 'dev', split_axis=0, concat_axis=0, tiled=True)  4.21 us
  transfers between devices with their start and end apart: 2, of which 2 were waited for; matrix products, arithmetic and copies ran while one was open for 8% of the time, Pallas kernels for 0%

commit v1 on v0

v1 whole, which is shorter than its diff:
```python
import functools

import jax
import jax.numpy as jnp
from jax import lax
from jax.experimental import pallas as pl
from jax.experimental.pallas import tpu as pltpu
from jax.sharding import PartitionSpec as P

LEARN_RATE = 0.001
DECAY_RATE = 0.1
BETA_ONE = 0.9
BETA_TWO = 0.95
BIAS_ONE = 1.0 - 0.9**20
BIAS_TWO = 1.0 - 0.95**20
EPSILON = 1e-08
GROUP = 8
CHUNKS = 4
MOST = 8
MESH = pl.DeviceIdType.MESH


def contract_rows(left, right):
    return lax.dot_general(
        left, right, (((0,), (0,)), ((), ())), preferred_element_type=jnp.float32
    )


def contract_cols(left, right):
    return lax.dot_general(
        left, right, (((1,), (1,)), ((), ())), preferred_element_type=jnp.float32
    )


def adam(grads, master, moment1, moment2):
    first = BETA_ONE * moment1 + (1.0 - BETA_ONE) * grads
    second = BETA_TWO * moment2 + (1.0 - BETA_TWO) * grads * grads
    update = first / BIAS_ONE / (jnp.sqrt(second / BIAS_TWO) + EPSILON) + DECAY_RATE * master
    return master - LEARN_RATE * update, first, second


def plain(saved, cotangent, weights, counts, live_rows, next_map, master, moment1, moment2):
    hidden_rows, cot_rows, slot_weights = saved[0], cotangent[0], weights[0]
    devices = lax.axis_size("dev")
    expert_count, share_rows, model_width = master.shape
    row_index = jnp.arange(hidden_rows.shape[0], dtype=jnp.int32)
    masked = jnp.where((row_index < live_rows[0])[:, None], cot_rows, jnp.zeros_like(cot_rows))
    input_grads = contract_cols(masked, slot_weights).astype(jnp.bfloat16)
    slot_grads = contract_rows(hidden_rows, masked).astype(jnp.bfloat16)
    slot_index = jnp.arange(devices, dtype=jnp.int32)
    bounds = jnp.cumsum(counts)
    holders = jnp.sum((bounds[None, :] <= slot_index[:, None]).astype(jnp.int32), axis=1)
    selector = (jnp.arange(expert_count, dtype=jnp.int32)[:, None] == holders[None, :]).astype(
        jnp.bfloat16
    )
    received = lax.all_to_all(slot_grads, "dev", split_axis=0, concat_axis=0, tiled=True)
    pieces = received.reshape(devices, share_rows, model_width)
    expert_grads = jnp.einsum("es,src->erc", selector, pieces, preferred_element_type=jnp.float32)
    master_out, first, second = adam(
        expert_grads, master, moment1.astype(jnp.float32), moment2.astype(jnp.float32)
    )
    outgoing = jnp.take(master_out.astype(jnp.bfloat16), next_map, axis=0)
    outgoing = outgoing.reshape(devices * share_rows, model_width)
    arriving = lax.all_to_all(outgoing, "dev", split_axis=0, concat_axis=0, tiled=True)
    return (
        input_grads[None],
        master_out,
        first.astype(jnp.bfloat16),
        second.astype(jnp.bfloat16),
        arriving[None],
    )


def tables(counts, next_map, devices):
    planes, experts = devices // GROUP, counts.shape[0]
    lane = jnp.arange(GROUP, dtype=jnp.int32)
    slot = jnp.arange(devices, dtype=jnp.int32)
    ids = jnp.arange(experts, dtype=jnp.int32)
    bounds = jnp.sum(jnp.where(ids[None, :] <= ids[:, None], counts[None, :], 0), axis=1)
    holders = jnp.sum((bounds[None, :] <= slot[:, None]).astype(jnp.int32), axis=1)
    held = holders.reshape(planes, GROUP)
    same = held[:, :, None] == held[:, None, :]
    earlier = lane[None, :] < lane[:, None]
    cont = jnp.any(same & earlier[None], axis=2)
    rank = jnp.sum((~cont[:, None, :]) & (lane[None, :] <= lane[:, None])[None], axis=2) - 1
    at_rank = rank[:, None, :] == lane[None, :, None]
    last = jnp.max(jnp.where(at_rank, lane[None, None, :], 0), axis=2)
    begin, end = bounds - counts, bounds - 1
    flat = rank.reshape(devices)
    rank_of = lambda s: jnp.sum(jnp.where(s[:, None] == slot[None, :], flat[None, :], 0), axis=1)
    upcoming = next_map.reshape(planes, GROUP)
    same = upcoming[:, :, None] == upcoming[:, None, :]
    again = jnp.any(same & earlier[None], axis=2)
    place = jnp.sum((~again[:, None, :]) & (lane[None, :] <= lane[:, None])[None], axis=2) - 1
    where = jnp.sum(jnp.where(same & ~again[:, None, :], place[:, None, :], 0), axis=2)
    at_place = (place[:, None, :] == lane[None, :, None]) & ~again[:, None, :]
    wanted = jnp.sum(jnp.where(at_place, upcoming[:, None, :], 0), axis=2)
    table = jnp.concatenate(
        [
            cont.astype(jnp.int32).reshape(-1),
            last.reshape(-1),
            where.reshape(-1),
            wanted.reshape(-1),
            begin // GROUP,
            rank_of(begin),
            end // GROUP,
            rank_of(end),
        ]
    ).astype(jnp.int32)
    return table, jnp.max(rank) + 1, jnp.max(place) + 1


def kernel(
    planes, most_now, most_next,
    table, live, saved, cot, weights, master, moment1, moment2,
    ig_out, master_out, moment1_out, moment2_out, next_out,
    saved_v, saved_t, cot_v, weights_v, master_v, moment1_v, moment2_v, ig_v, next_v,
    grad_v, sums, fresh, now_v, later_v, xy_s, xy_r, z_s, z_r, nz_s, nz_r, nxy_s, nxy_r,
    load_sem, s1, r1, s2, r2, s3, r3, s4, r4,
):
    me = lax.axis_index("dev")
    plane, spot = me // GROUP, lax.rem(me, GROUP)
    devices = planes * GROUP
    experts, share, width = master_v.shape
    rows, hidden = saved_v.shape
    wide = width // CHUNKS
    f32, bf16 = jnp.float32, jnp.bfloat16

    loads = [
        pltpu.make_async_copy(a, b, load_sem.at[i])
        for i, (a, b) in enumerate(
            [
                (saved, saved_v), (cot, cot_v), (weights, weights_v),
                (master, master_v), (moment1, moment1_v), (moment2, moment2_v),
            ]
        )
    ]
    for load in loads:
        load.start()

    barrier = pltpu.get_barrier_semaphore()
    peers = [plane * GROUP + lax.rem(spot + o, GROUP) for o in range(1, GROUP)]
    peers += [lax.rem(plane + o, planes) * GROUP + spot for o in range(1, planes)]
    for peer in peers:
        pl.semaphore_signal(barrier, inc=1, device_id=(peer,), device_id_type=MESH)
    pl.semaphore_wait(barrier, len(peers))

    def exchange(src, dst, ssem, rsem, mine, count, device_of):
        def remote(c, other, slot):
            return pltpu.make_async_remote_copy(
                src_ref=src.at[c, other], dst_ref=dst.at[c, slot],
                send_sem=ssem.at[c, other], recv_sem=rsem.at[c, slot],
                device_id=(device_of(other),), device_id_type=MESH,
            )

        def own(c):
            return pltpu.make_async_copy(src.at[c, mine], dst.at[c, mine], rsem.at[c, mine])

        others = [lax.rem(mine + o, count) for o in range(1, count)]

        def send(c):
            for other in others:
                remote(c, other, mine).start()
            own(c).start()

        def arrived(c):
            for other in others:
                remote(c, other, other).wait_recv()
            own(c).wait()

        def sent(c):
            for other in others:
                remote(c, other, mine).wait_send()

        return send, arrived, sent

    in_plane = lambda s: plane * GROUP + s
    along_z = lambda p: p * GROUP + spot
    send_xy, arrived_xy, sent_xy = exchange(xy_s, xy_r, s1, r1, spot, GROUP, in_plane)
    send_z, arrived_z, sent_z = exchange(z_s, z_r, s2, r2, plane, planes, along_z)
    send_nz, arrived_nz, sent_nz = exchange(nz_s, nz_r, s3, r3, plane, planes, along_z)
    send_nxy, arrived_nxy, sent_nxy = exchange(nxy_s, nxy_r, s4, r4, spot, GROUP, in_plane)

    def columns(c):
        return pl.ds(pl.multiple_of(c * wide, wide), wide)

    live_count = live[0]
    loads[0].wait()
    step = 256
    for t in range(rows // step):
        index = lax.broadcasted_iota(jnp.int32, (step, hidden), 0) + t * step
        part = saved_v[t * step : (t + 1) * step, :].astype(f32)
        part = jnp.where(index < live_count, part, 0.0)
        saved_t[:, t * step : (t + 1) * step] = part.T.astype(bf16)

    loads[1].wait()

    @pl.loop(0, CHUNKS)
    def _(c):
        grad_v[...] = jnp.dot(saved_t[...], cot_v[:, columns(c)], preferred_element_type=f32)
        for s in range(GROUP):
            parts = [
                grad_v[(p * GROUP + s) * share : (p * GROUP + s + 1) * share, :]
                for p in range(planes)
            ]
            xy_s[c, s] = jnp.concatenate(parts, axis=0).astype(bf16)
        send_xy(c)

    loads[2].wait()

    @pl.loop(0, rows // step)
    def _(t):
        at = pl.ds(pl.multiple_of(t * step, step), step)
        index = lax.broadcasted_iota(jnp.int32, (step, hidden), 0) + t * step
        out = contract_cols(cot_v[at, :], weights_v[...])
        ig_v[at, :] = jnp.where(index < live_count, out, 0.0).astype(bf16)

    ig_store = pltpu.make_async_copy(ig_v, ig_out, load_sem.at[6])
    ig_store.start()

    @pl.loop(0, CHUNKS)
    def _(c):
        arrived_xy(c)
        for p in range(planes):
            total = jnp.zeros((share, wide), f32)
            for s in range(GROUP):
                keep = table[plane * GROUP + s].astype(f32)
                fresh_part = xy_r[c, s].astype(f32)[p * share : (p + 1) * share, :]
                total = total * keep + fresh_part
                sums[p, s] = total.astype(bf16)
            for k in range(most_now):
                z_s[c, p, k] = sums[p, table[devices + plane * GROUP + k]]
        send_z(c)

    for load in loads[3:]:
        load.wait()
    base = 4 * devices

    def scatter(c):
        arrived_nz(c)
        for p in range(planes):
            for k in range(most_next):
                later_v[p, k] = nz_r[c, p, k]
        for s in range(GROUP):
            place = table[2 * devices + plane * GROUP + s]
            parts = [later_v[p, place].astype(f32) for p in range(planes)]
            nxy_s[c, s] = jnp.concatenate(parts, axis=0).astype(bf16)
        send_nxy(c)

    @pl.loop(0, CHUNKS + 1)
    def _(c):
        @pl.when(c < CHUNKS)
        def _():
            arrived_z(c)
            cols = columns(c)
            for p in range(planes):
                for k in range(most_now):
                    now_v[p, k] = z_r[c, p, k]

            @pl.loop(0, experts)
            def _(e):
                begin = now_v[table[base + e], table[base + experts + e]]
                end = now_v[table[base + 2 * experts + e], table[base + 3 * experts + e]]
                split = (table[base + e] != table[base + 2 * experts + e]).astype(f32)
                grads = begin.astype(f32) + split * end.astype(f32)
                new, one, two = adam(
                    grads,
                    master_v[e, :, cols],
                    moment1_v[e, :, cols].astype(f32),
                    moment2_v[e, :, cols].astype(f32),
                )
                master_v[e, :, cols] = new
                moment1_v[e, :, cols] = one.astype(bf16)
                moment2_v[e, :, cols] = two.astype(bf16)
                fresh[e] = new.astype(bf16)

            for p in range(planes):
                for k in range(most_next):
                    nz_s[c, p, k] = fresh[table[3 * devices + p * GROUP + k]]
            send_nz(c)

        @pl.when(c > 0)
        def _():
            scatter(c - 1)

    stores = [
        pltpu.make_async_copy(a, b, load_sem.at[7 + i])
        for i, (a, b) in enumerate(
            [(master_v, master_out), (moment1_v, moment1_out), (moment2_v, moment2_out)]
        )
    ]
    for store in stores:
        store.start()

    @pl.loop(0, CHUNKS)
    def _(c):
        arrived_nxy(c)
        for p in range(planes):
            for s in range(0, GROUP, 2):
                pair = [
                    nxy_r[c, s + i].astype(f32)[p * share : (p + 1) * share, :] for i in range(2)
                ]
                at = (p * GROUP + s) * share
                next_v[at : at + 2 * share, columns(c)] = jnp.concatenate(pair, axis=0).astype(bf16)

    store = pltpu.make_async_copy(next_v, next_out, load_sem.at[10])
    store.start()

    @pl.loop(0, CHUNKS)
    def _(c):
        for sent in (sent_xy, sent_z, sent_nz, sent_nxy):
            sent(c)

    for done in [ig_store] + stores + [store]:
        done.wait()


def fused(most_now, most_next, number, table, live, saved, cot, weights, master, moment1, moment2):
    devices = lax.axis_size("dev")
    planes = devices // GROUP
    experts, share, width = master.shape
    rows, hidden = saved.shape
    wide = width // CHUNKS
    bf16, f32 = jnp.bfloat16, jnp.float32
    vmem = pltpu.VMEM
    dma = pltpu.SemaphoreType.DMA
    anywhere = pl.BlockSpec(memory_space=pl.ANY)
    scalars = pl.BlockSpec(memory_space=pltpu.SMEM)
    across = vmem((CHUNKS, GROUP, planes * share, wide), bf16)
    now = vmem((CHUNKS, planes, most_now, share, wide), bf16)
    later = vmem((CHUNKS, planes, most_next, share, wide), bf16)
    return pl.pallas_call(
        functools.partial(kernel, planes, most_now, most_next),
        out_shape=(
            jax.ShapeDtypeStruct((rows, hidden), bf16),
            jax.ShapeDtypeStruct(master.shape, f32),
            jax.ShapeDtypeStruct(moment1.shape, bf16),
            jax.ShapeDtypeStruct(moment2.shape, bf16),
            jax.ShapeDtypeStruct((hidden, width), bf16),
        ),
        in_specs=[scalars] * 2 + [anywhere] * 6,
        out_specs=(anywhere,) * 5,
        scratch_shapes=[
            vmem((rows, hidden), bf16),
            vmem((hidden, rows), bf16),
            vmem((rows, width), bf16),
            vmem((hidden, width), bf16),
            vmem(master.shape, f32),
            vmem(moment1.shape, bf16),
            vmem(moment2.shape, bf16),
            vmem((rows, hidden), bf16),
            vmem((hidden, width), bf16),
            vmem((hidden, wide), f32),
            vmem((planes, GROUP, share, wide), bf16),
            vmem((experts, share, wide), bf16),
            vmem((planes, most_now, share, wide), bf16),
            vmem((planes, most_next, share, wide), bf16),
            across, across, now, now, later, later, across, across,
            dma((11,)),
            dma((CHUNKS, GROUP)), dma((CHUNKS, GROUP)),
            dma((CHUNKS, planes)), dma((CHUNKS, planes)),
            dma((CHUNKS, planes)), dma((CHUNKS, planes)),
            dma((CHUNKS, GROUP)), dma((CHUNKS, GROUP)),
        ],
        compiler_params=pltpu.CompilerParams(
            collective_id=number, has_side_effects=True, vmem_limit_bytes=58 * 1024 * 1024
        ),
        cost_estimate=pl.CostEstimate(
            flops=4 * rows * hidden * width, bytes_accessed=26 << 20, transcendentals=0
        ),
        name=f"moe_step_{most_now}_{most_next}",
    )(table, live, saved, cot, weights, master, moment1, moment2)


def exchanged(saved, cotangent, weights, counts, live_rows, next_map, master, moment1, moment2):
    table, now, later = tables(counts, next_map, lax.axis_size("dev"))
    args = (table, live_rows, saved[0], cotangent[0], weights[0], master, moment1, moment2)
    few = GROUP - 1
    fits = (now <= few) & (later <= few)
    outs = lax.cond(
        fits,
        functools.partial(fused, few, few, 0),
        functools.partial(fused, GROUP, GROUP, 1),
        *args,
    )
    return (outs[0][None], outs[1], outs[2], outs[3], outs[4][None])


def solution(mesh):
    devices = mesh.shape["dev"]

    def per_device(*args):
        share, width = args[6].shape[1:]
        takes = devices % GROUP == 0 and GROUP >= MOST and share % 8 == 0
        takes = takes and width % (CHUNKS * 128) == 0 and args[0].shape[1] % 256 == 0
        return (exchanged if takes else plain)(*args)

    placed = (
        P("dev", None, None),
        P("dev", None, None),
        P("dev", None, None),
        P(),
        P("dev"),
        P(),
        P(None, "dev", None),
        P(None, "dev", None),
        P(None, "dev", None),
    )
    return jax.shard_map(
        per_device,
        mesh=mesh,
        in_specs=placed,
        out_specs=(
            P("dev", None, None),
            P(None, "dev", None),
            P(None, "dev", None),
            P(None, "dev", None),
            P("dev", None, None),
        ),
        check_vma=False,
    )
```

time: 197 us -> 166 us (0.84)
  Pallas kernels: 0 us -> 147 us
  waiting for transfers between devices: 128 us -> 0 us
  matrix products: 33.7 us -> 0 us
  starting transfers between devices: 11.8 us -> 0 us
  local copies, waits for them, and re-layouts: 17.4 us -> 11.1 us
    pallas_call x0 -> x1, Pallas kernels: none -> 147 us  [fused(): pl.pallas_call(functools.partial(kernel, planes, most_now, most_next), ou...]
    all_to_all x2 -> x0, waiting for transfers between devices: 128 us -> none  [the longest x1 71 us: per_device(): lax.all_to_all(slot_grads, 'dev', split_axis=0, concat_axis=0, tiled=True)]
    dot_general x3 -> x0, matrix products: 33.7 us -> none  [the longest x1 18.7 us: per_device(): jnp.einsum('es,src->erc', selector, pieces, preferred_element_type=jnp.fl...]
    all_to_all x2 -> x0, starting transfers between devices: 11.8 us -> none  [the longest x1 7.59 us: per_device(): lax.all_to_all(slot_grads, 'dev', split_axis=0, concat_axis=0, tiled=True)]
    gather x1 -> x0, local copies, waits for them, and re-layouts: 3.82 us -> none  [per_device(): jnp.take(master_out.astype(jnp.bfloat16), next_map, axis=0)]
    select_n x2 -> x1, other arithmetic: 3.94 us -> 0.67 us  [tables(): end // GROUP]
    unnamed x16 -> x11, local copies, waits for them, and re-layouts: 11.5 us -> 9.78 us
  transfers between devices with their start and end apart: 2 -> 0, of which waited for: 2 -> 0; matrix products, arithmetic and copies ran while one was open for 8% -> 0% of each run, Pallas kernels for 0% -> 0%
where the time goes in v1:
time: 166 us; the launch traced here: 164 us
  Pallas kernels  147 us (89%)
  local copies, waits for them, and re-layouts  11.1 us (7%)
  other arithmetic  3.29 us (2%)
  between operations  1.99 us (1%)
    pallas_call x1, Pallas kernels, fused(): pl.pallas_call(functools.partial(kernel, planes, most_now, most_next), ou...  147 us
    unnamed x11, local copies, waits for them, and re-layouts  9.78 us

profile of v1, /device:TPU:0, one launch (start us, length us, event | category | flops | bytes accessed | tf_op | source)
XLA Modules:
  0.0 163.7 jit_solution(3826355227826997214)
XLA Ops:
  0.6 0.8 select_reduce_fusion.5
  1.4 0.1 convert_reduce_fusion.2
  1.5 0.1 eq.38
  1.6 0.7 and_select_fusion
  2.3 0.7 eq.84
  3.0 0.3 fusion.1
  3.3 0.1 reshape.81
  3.4 0.2 convert_reduce_fusion
  3.6 0.6 broadcast_add_fusion
  5.6 0.2 select_reduce_fusion
  5.8 0.1 reshape.80
  5.9 0.1 reshape.79
  6.0 0.1 sub.25
  6.1 0.2 select_reduce_fusion.3
  6.3 0.2 select_reduce_fusion.2
  6.4 0.1 reshape.78
  6.5 0.1 concatenate.3
  6.6 147.4 %conditional.1 = ((bf16[1024,768]{1,0:T(8,128)(2,1)S(1)}, f32[16,24,2048]{2,1,0:T(8,128)S(1)}, bf16[16,24,2048]{2,1,0:T(8,128)(2,1)}, bf16[16,24,2048]{2,1,0:T(8,128)(2,1)}, bf16[768,2048]{1,0:T(8,128)(2,1)})) conditional(s32[]{:T(128)} %convert_element_type.22, (bf16[1,1024,768]{2,1,0:T(8,128)(2,1)}, bf16[1,1024,2048]{2,1,0:T(8,128)(2,1)}, ...), branch_computations={%region_13.14_spmd, %region_14.15_spmd} | conditional | flops 6442450944 | bytes 27262984 | solution.py:380
  6.6 147.4 %moe_step_7_7.1 = (bf16[1024,768]{1,0:T(8,128)(2,1)S(1)}, f32[16,24,2048]{2,1,0:T(8,128)S(1)}, bf16[16,24,2048]{2,1,0:T(8,128)(2,1)}, bf16[16,24,2048]{2,1,0:T(8,128)(2,1)}, bf16[768,2048]{1,0:T(8,128)(2,1)}) custom-call(s32[192]{0:T(256)S(1)} %get-tuple-element.64.table, s32[1]{0:T(128)} %get-tuple-element.120.live, bf16[1024,768]{1,0:T(8,128)(2,1)} %bitcast.15, ...), custom_call_target="tpu_custom_call" | custom-call | flops 6442450944 | bytes 27262976 | tf_op jit(solution)/shard_map/cond/branch_1_fun/moe_step_7_7/pallas_call | solution.py:332
  153.9 1.1 copy.43
  155.1 0.0 copy-start.1
  155.1 1.7 %copy.44 = f32[16,24,2048]{2,1,0:T(8,128)} copy(f32[16,24,2048]{2,1,0:T(8,128)S(1)} %get-tuple-element.173) | data formatting | bytes 6291456
  156.8 0.9 copy-done.1
  157.6 0.0 copy-start.2
  157.6 1.1 copy.45
  158.8 0.8 copy-done.2
  159.6 0.0 copy-start
  159.6 1.1 copy.46
  160.8 1.3 copy-done
  162.1 1.7 %copy.47 = bf16[1,768,2048]{2,1,0:T(8,128)(2,1)} copy(bf16[1,768,2048]{2,1,0:T(8,128)(2,1)S(1)} %bitcast.8) | data formatting | bytes 6291456
  (4 shorter events, 0.0 us)
Async XLA Ops:
  155.1 2.5 %copy-start.1 = (bf16[16,24,2048]{2,1,0:T(8,128)(2,1)S(1)}, bf16[16,24,2048]{2,1,0:T(8,128)(2,1)}, u32[]{:S(2)}) copy-start(bf16[16,24,2048]{2,1,0:T(8,128)(2,1)} %get-tuple-element.174) | copy-start | bytes 4718596
  157.6 2.0 %copy-start.2 = (bf16[16,24,2048]{2,1,0:T(8,128)(2,1)S(1)}, bf16[16,24,2048]{2,1,0:T(8,128)(2,1)}, u32[]{:S(2)}) copy-start(bf16[16,24,2048]{2,1,0:T(8,128)(2,1)} %get-tuple-element.175) | copy-start | bytes 4718596
  159.6 2.5 %copy-start = (bf16[768,2048]{1,0:T(8,128)(2,1)S(1)}, bf16[768,2048]{1,0:T(8,128)(2,1)}, u32[]{:S(2)}) copy-start(bf16[768,2048]{1,0:T(8,128)(2,1)} %get-tuple-element.128) | copy-start | bytes 9437188

commit v2 on v1

--- a/solution.py
+++ b/solution.py
@@ -15,8 +15,10 @@
 BIAS_TWO = 1.0 - 0.95**20
 EPSILON = 1e-08
 GROUP = 8
-CHUNKS = 4
+CHUNKS = 8
+PLANES = 4
 MOST = 8
+FEW = 12
 MESH = pl.DeviceIdType.MESH
 
 
@@ -72,55 +74,49 @@
 
 
 def tables(counts, next_map, devices):
-    planes, experts = devices // GROUP, counts.shape[0]
-    lane = jnp.arange(GROUP, dtype=jnp.int32)
+    experts = counts.shape[0]
     slot = jnp.arange(devices, dtype=jnp.int32)
     ids = jnp.arange(experts, dtype=jnp.int32)
-    bounds = jnp.sum(jnp.where(ids[None, :] <= ids[:, None], counts[None, :], 0), axis=1)
+    upto = ids[None, :] <= ids[:, None]
+    bounds = jnp.sum(jnp.where(upto, counts[None, :], 0), axis=1)
     holders = jnp.sum((bounds[None, :] <= slot[:, None]).astype(jnp.int32), axis=1)
-    held = holders.reshape(planes, GROUP)
-    same = held[:, :, None] == held[:, None, :]
-    earlier = lane[None, :] < lane[:, None]
-    cont = jnp.any(same & earlier[None], axis=2)
-    rank = jnp.sum((~cont[:, None, :]) & (lane[None, :] <= lane[:, None])[None], axis=2) - 1
-    at_rank = rank[:, None, :] == lane[None, :, None]
-    last = jnp.max(jnp.where(at_rank, lane[None, None, :], 0), axis=2)
-    begin, end = bounds - counts, bounds - 1
-    flat = rank.reshape(devices)
-    rank_of = lambda s: jnp.sum(jnp.where(s[:, None] == slot[None, :], flat[None, :], 0), axis=1)
-    upcoming = next_map.reshape(planes, GROUP)
-    same = upcoming[:, :, None] == upcoming[:, None, :]
-    again = jnp.any(same & earlier[None], axis=2)
-    place = jnp.sum((~again[:, None, :]) & (lane[None, :] <= lane[:, None])[None], axis=2) - 1
-    where = jnp.sum(jnp.where(same & ~again[:, None, :], place[:, None, :], 0), axis=2)
-    at_place = (place[:, None, :] == lane[None, :, None]) & ~again[:, None, :]
-    wanted = jnp.sum(jnp.where(at_place, upcoming[:, None, :], 0), axis=2)
+    half = devices // 2
+    upcoming = next_map.reshape(2, 1, half)
+    present = jnp.max((upcoming == ids[None, :, None]).astype(jnp.int32), axis=2)
+    place = jnp.sum(jnp.where(upto[None], present[:, None, :], 0), axis=2) - 1
+    at = (place[:, None, :] == jnp.arange(half, dtype=jnp.int32)[None, :, None]) & (
+        present[:, None, :] > 0
+    )
+    union = jnp.sum(jnp.where(at, ids[None, None, :], 0), axis=2)
     table = jnp.concatenate(
-        [
-            cont.astype(jnp.int32).reshape(-1),
-            last.reshape(-1),
-            where.reshape(-1),
-            wanted.reshape(-1),
-            begin // GROUP,
-            rank_of(begin),
-            end // GROUP,
-            rank_of(end),
-        ]
+        [bounds, holders, next_map, place.reshape(-1), union.reshape(-1)]
     ).astype(jnp.int32)
-    return table, jnp.max(rank) + 1, jnp.max(place) + 1
+    held = jnp.maximum(holders[half - 1] - holders[0], holders[devices - 1] - holders[half])
+    return table, jnp.maximum(held, jnp.maximum(place[0, -1], place[1, -1])) + 1
 
 
 def kernel(
-    planes, most_now, most_next,
+    most,
     table, live, saved, cot, weights, master, moment1, moment2,
     ig_out, master_out, moment1_out, moment2_out, next_out,
     saved_v, saved_t, cot_v, weights_v, master_v, moment1_v, moment2_v, ig_v, next_v,
-    grad_v, sums, fresh, now_v, later_v, xy_s, xy_r, z_s, z_r, nz_s, nz_r, nxy_s, nxy_r,
-    load_sem, s1, r1, s2, r2, s3, r3, s4, r4,
+    grad_v, sums, fresh, own_v, half_v, mate_v, cross_v, union_v, gather_v,
+    xy_s, xy_r, half_s, half_r, mate_s, mate_r, cross_s, cross_r,
+    union_s, union_r, back_s, back_r, pass_s, pass_r, nxy_s, nxy_r,
+    load_sem, s1, r1, s2, r2, s4, r4,
 ):
     me = lax.axis_index("dev")
     plane, spot = me // GROUP, lax.rem(me, GROUP)
-    devices = planes * GROUP
+    planes, devices = PLANES, PLANES * GROUP
+    side = plane // 2
+    inner = 1 + side
+    is_inner = plane == inner
+    mate = 2 * side + 1 - lax.rem(plane, 2)
+    far = 1 - side
+    far_inner, far_outer = 2 - side, 3 - 3 * side
+    at_mate, at_far_inner, at_far_outer = (
+        p * GROUP + spot for p in (mate, far_inner, far_outer)
+    )
     experts, share, width = master_v.shape
     rows, hidden = saved_v.shape
     wide = width // CHUNKS
@@ -175,11 +171,45 @@
         return send, arrived, sent
 
     in_plane = lambda s: plane * GROUP + s
-    along_z = lambda p: p * GROUP + spot
     send_xy, arrived_xy, sent_xy = exchange(xy_s, xy_r, s1, r1, spot, GROUP, in_plane)
-    send_z, arrived_z, sent_z = exchange(z_s, z_r, s2, r2, plane, planes, along_z)
-    send_nz, arrived_nz, sent_nz = exchange(nz_s, nz_r, s3, r3, plane, planes, along_z)
     send_nxy, arrived_nxy, sent_nxy = exchange(nxy_s, nxy_r, s4, r4, spot, GROUP, in_plane)
+
+    def along(c, number, src, dst, device):
+        return pltpu.make_async_remote_copy(
+            src_ref=src, dst_ref=dst, send_sem=s2.at[c, number], recv_sem=r2.at[c, number],
+            device_id=(device,), device_id_type=MESH,
+        )
+
+    def to_mate(c):
+        return along(c, 0, mate_s.at[c], mate_r.at[c], at_mate)
+
+    def half_to_mate(c):
+        return along(c, 1, half_s.at[c], half_r.at[c], at_mate)
+
+    def across_inner(c):
+        return along(c, 2, cross_s.at[c, 0], cross_r.at[c], at_far_inner)
+
+    def across_outer(c):
+        return pltpu.make_async_remote_copy(
+            src_ref=cross_s.at[c, 1], dst_ref=cross_r.at[c],
+            send_sem=s2.at[c, 3], recv_sem=r2.at[c, 2],
+            device_id=(at_far_outer,), device_id_type=MESH,
+        )
+
+    def union_to_far(c, slot):
+        return pltpu.make_async_remote_copy(
+            src_ref=union_s.at[c], dst_ref=union_r.at[c, slot],
+            send_sem=s2.at[c, 4], recv_sem=r2.at[c, 3 + slot],
+            device_id=(at_far_inner,), device_id_type=MESH,
+        )
+
+    def back_to_mate(c):
+        return along(c, 5, back_s.at[c], back_r.at[c], at_mate)
+
+    def pass_to_mate(c):
+        return along(c, 6, pass_s.at[c], pass_r.at[c], at_mate)
+
+    parity = lax.rem(plane, 2)
 
     def columns(c):
         return pl.ds(pl.multiple_of(c * wide, wide), wide)
@@ -218,70 +248,156 @@
     ig_store = pltpu.make_async_copy(ig_v, ig_out, load_sem.at[6])
     ig_store.start()
 
-    @pl.loop(0, CHUNKS)
-    def _(c):
-        arrived_xy(c)
-        for p in range(planes):
-            total = jnp.zeros((share, wide), f32)
-            for s in range(GROUP):
-                keep = table[plane * GROUP + s].astype(f32)
-                fresh_part = xy_r[c, s].astype(f32)[p * share : (p + 1) * share, :]
-                total = total * keep + fresh_part
-                sums[p, s] = total.astype(bf16)
-            for k in range(most_now):
-                z_s[c, p, k] = sums[p, table[devices + plane * GROUP + k]]
-        send_z(c)
-
-    for load in loads[3:]:
-        load.wait()
-    base = 4 * devices
-
-    def scatter(c):
-        arrived_nz(c)
-        for p in range(planes):
-            for k in range(most_next):
-                later_v[p, k] = nz_r[c, p, k]
-        for s in range(GROUP):
-            place = table[2 * devices + plane * GROUP + s]
-            parts = [later_v[p, place].astype(f32) for p in range(planes)]
-            nxy_s[c, s] = jnp.concatenate(parts, axis=0).astype(bf16)
-        send_nxy(c)
+    holder_at, next_at = experts, experts + devices
+    place_at = experts + 2 * devices
+    union_at = 3 * experts + 2 * devices
+
+    def span(first_slot, slots):
+        return table[holder_at + first_slot], table[holder_at + first_slot + slots - 1]
+
+    def taken(e, held, most_held):
+        first, last = held
+        here = jnp.where(e >= first, 1.0, 0.0) * jnp.where(e <= last, 1.0, 0.0)
+        return jnp.clip(e - first, 0, most_held - 1), here
+
+    held_own = span(plane * GROUP, GROUP)
+    held_mate = span(mate * GROUP, GROUP)
+    held_side = span(side * 2 * GROUP, 2 * GROUP)
+    held_far = span(far * 2 * GROUP, 2 * GROUP)
+
+    def combine(c):
+        half_to_mate(c).wait_recv()
+        for i in range(2):
+            for k in range(GROUP):
+                half_v[i, k] = half_r[c, i, k]
+
+        @pl.loop(0, most)
+        def _(q):
+            e = held_side[0] + q
+            mine, mine_here = taken(e, held_own, GROUP)
+            theirs, theirs_here = taken(e, held_mate, GROUP)
+            for i in range(2):
+                total = half_s[c, i, mine].astype(f32) * mine_here
+                total = total + half_v[i, theirs].astype(f32) * theirs_here
+                cross_s[c, i, q] = total.astype(bf16)
+
+        across_inner(c).start()
+        across_outer(c).start()
 
     @pl.loop(0, CHUNKS + 1)
     def _(c):
         @pl.when(c < CHUNKS)
         def _():
-            arrived_z(c)
-            cols = columns(c)
+            arrived_xy(c)
             for p in range(planes):
-                for k in range(most_now):
-                    now_v[p, k] = z_r[c, p, k]
-
-            @pl.loop(0, experts)
-            def _(e):
-                begin = now_v[table[base + e], table[base + experts + e]]
-                end = now_v[table[base + 2 * experts + e], table[base + 3 * experts + e]]
-                split = (table[base + e] != table[base + 2 * experts + e]).astype(f32)
-                grads = begin.astype(f32) + split * end.astype(f32)
-                new, one, two = adam(
-                    grads,
-                    master_v[e, :, cols],
-                    moment1_v[e, :, cols].astype(f32),
-                    moment2_v[e, :, cols].astype(f32),
-                )
-                master_v[e, :, cols] = new
-                moment1_v[e, :, cols] = one.astype(bf16)
-                moment2_v[e, :, cols] = two.astype(bf16)
-                fresh[e] = new.astype(bf16)
-
-            for p in range(planes):
-                for k in range(most_next):
-                    nz_s[c, p, k] = fresh[table[3 * devices + p * GROUP + k]]
-            send_nz(c)
-
-        @pl.when(c > 0)
-        def _():
+                total = jnp.zeros((share, wide), f32)
+                for s in range(GROUP):
+                    now = plane * GROUP + s
+                    if s:
+                        same = table[holder_at + now] == table[holder_at + now - 1]
+                        total = total * jnp.where(same, 1.0, 0.0)
+                    total = total + xy_r[c, s].astype(f32)[p * share : (p + 1) * share, :]
+                    sums[p, s] = total.astype(bf16)
+            for k in range(GROUP):
+                e = jnp.minimum(held_own[0] + k, experts - 1)
+                last = jnp.clip(table[e] - 1 - plane * GROUP, 0, GROUP - 1)
+                half_s[c, 0, k] = sums[far_inner, last]
+                half_s[c, 1, k] = sums[far_outer, last]
+                mate_s[c, k] = sums[mate, last]
+                own_v[c, k] = sums[plane, last]
+
+            @pl.when(jnp.logical_not(is_inner))
+            def _():
+                half_to_mate(c).start()
+
+            to_mate(c).start()
+
+        @pl.when((c > 0) & is_inner)
+        def _():
+            combine(c - 1)
+
+    for load in loads[3:]:
+        load.wait()
+
+    def update(c):
+        to_mate(c).wait_recv()
+        across_inner(c).wait_recv()
+        for k in range(GROUP):
+            mate_v[k] = mate_r[c, k]
+        for k in range(most):
+            cross_v[k] = cross_r[c, k]
+        cols = columns(c)
+
+        @pl.loop(0, experts)
+        def _(e):
+            at_own, own_here = taken(e, held_own, GROUP)
+            at_next, next_here = taken(e, held_mate, GROUP)
+            at_far, far_here = taken(e, held_far, most)
+            grads = own_v[c, at_own].astype(f32) * own_here
+            grads = grads + mate_v[at_next].astype(f32) * next_here
+            grads = grads + cross_v[at_far].astype(f32) * far_here
+            new, one, two = adam(
+                grads,
+                master_v[e, :, cols],
+                moment1_v[e, :, cols].astype(f32),
+                moment2_v[e, :, cols].astype(f32),
+            )
+            master_v[e, :, cols] = new
+            moment1_v[e, :, cols] = one.astype(bf16)
+            moment2_v[e, :, cols] = two.astype(bf16)
+            fresh[c, e] = new.astype(bf16)
+
+        for q in range(most):
+            union_s[c, q] = fresh[c, table[union_at + far * (devices // 2) + q]]
+        union_to_far(c, parity).start()
+        for s in range(GROUP):
+            back_s[c, s] = fresh[c, table[next_at + mate * GROUP + s]]
+        back_to_mate(c).start()
+
+    def hand_on(c):
+        for i in range(2):
+            union_to_far(c, i).wait_recv()
+        for i in range(2):
+            for q in range(most):
+                union_v[i, q] = union_r[c, i, q]
+        for s in range(GROUP):
+            place = table[place_at + side * experts + table[next_at + mate * GROUP + s]]
+            for i in range(2):
+                pass_s[c, i, s] = union_v[i, place]
+        pass_to_mate(c).start()
+        for s in range(GROUP):
+            place = table[place_at + side * experts + table[next_at + plane * GROUP + s]]
+            for i in range(2):
+                gather_v[2 * far + i, s] = union_v[i, place]
+
+    def scatter(c):
+        back_to_mate(c).wait_recv()
+        for s in range(GROUP):
+            gather_v[plane, s] = fresh[c, table[next_at + plane * GROUP + s]]
+            gather_v[mate, s] = back_r[c, s]
+        for s in range(GROUP):
+            parts = [gather_v[p, s].astype(f32) for p in range(planes)]
+            nxy_s[c, s] = jnp.concatenate(parts, axis=0).astype(bf16)
+        send_nxy(c)
+
+    @pl.loop(0, CHUNKS + 2)
+    def _(c):
+        @pl.when(c < CHUNKS)
+        def _():
+            update(c)
+
+        @pl.when((c > 0) & (c <= CHUNKS) & is_inner)
+        def _():
+            hand_on(c - 1)
             scatter(c - 1)
+
+        @pl.when((c > 1) & jnp.logical_not(is_inner))
+        def _():
+            pass_to_mate(c - 2).wait_recv()
+            for i in range(2):
+                for s in range(GROUP):
+                    gather_v[2 * far + i, s] = pass_r[c - 2, i, s]
+            scatter(c - 2)
 
     stores = [
         pltpu.make_async_copy(a, b, load_sem.at[7 + i])
@@ -308,16 +424,27 @@
 
     @pl.loop(0, CHUNKS)
     def _(c):
-        for sent in (sent_xy, sent_z, sent_nz, sent_nxy):
-            sent(c)
+        sent_xy(c)
+        to_mate(c).wait_send()
+        union_to_far(c, parity).wait_send()
+        back_to_mate(c).wait_send()
+        sent_nxy(c)
+
+        @pl.when(is_inner)
+        def _():
+            across_inner(c).wait_send()
+            across_outer(c).wait_send()
+            pass_to_mate(c).wait_send()
+
+        @pl.when(jnp.logical_not(is_inner))
+        def _():
+            half_to_mate(c).wait_send()
 
     for done in [ig_store] + stores + [store]:
         done.wait()
 
 
-def fused(most_now, most_next, number, table, live, saved, cot, weights, master, moment1, moment2):
-    devices = lax.axis_size("dev")
-    planes = devices // GROUP
+def fused(most, number, table, live, saved, cot, weights, master, moment1, moment2):
     experts, share, width = master.shape
     rows, hidden = saved.shape
     wide = width // CHUNKS
@@ -326,11 +453,10 @@
     dma = pltpu.SemaphoreType.DMA
     anywhere = pl.BlockSpec(memory_space=pl.ANY)
     scalars = pl.BlockSpec(memory_space=pltpu.SMEM)
-    across = vmem((CHUNKS, GROUP, planes * share, wide), bf16)
-    now = vmem((CHUNKS, planes, most_now, share, wide), bf16)
-    later = vmem((CHUNKS, planes, most_next, share, wide), bf16)
+    across = vmem((CHUNKS, GROUP, PLANES * share, wide), bf16)
+    blocks = lambda *lead: vmem((*lead, share, wide), bf16)
     return pl.pallas_call(
-        functools.partial(kernel, planes, most_now, most_next),
+        functools.partial(kernel, most),
         out_shape=(
             jax.ShapeDtypeStruct((rows, hidden), bf16),
             jax.ShapeDtypeStruct(master.shape, f32),
@@ -351,15 +477,21 @@
             vmem((rows, hidden), bf16),
             vmem((hidden, width), bf16),
             vmem((hidden, wide), f32),
-            vmem((planes, GROUP, share, wide), bf16),
-            vmem((experts, share, wide), bf16),
-            vmem((planes, most_now, share, wide), bf16),
-            vmem((planes, most_next, share, wide), bf16),
-            across, across, now, now, later, later, across, across,
+            blocks(PLANES, GROUP),
+            blocks(CHUNKS, experts),
+            blocks(CHUNKS, GROUP), blocks(2, GROUP), blocks(GROUP),
+            blocks(most), blocks(2, most), blocks(PLANES, GROUP),
+            across, across,
+            blocks(CHUNKS, 2, GROUP), blocks(CHUNKS, 2, GROUP),
+            blocks(CHUNKS, GROUP), blocks(CHUNKS, GROUP),
+            blocks(CHUNKS, 2, most), blocks(CHUNKS, most),
+            blocks(CHUNKS, most), blocks(CHUNKS, 2, most),
+            blocks(CHUNKS, GROUP), blocks(CHUNKS, GROUP),
+            blocks(CHUNKS, 2, GROUP), blocks(CHUNKS, 2, GROUP),
+            across, across,
             dma((11,)),
             dma((CHUNKS, GROUP)), dma((CHUNKS, GROUP)),
-            dma((CHUNKS, planes)), dma((CHUNKS, planes)),
-            dma((CHUNKS, planes)), dma((CHUNKS, planes)),
+            dma((CHUNKS, 7)), dma((CHUNKS, 7)),
             dma((CHUNKS, GROUP)), dma((CHUNKS, GROUP)),
         ],
         compiler_params=pltpu.CompilerParams(
@@ -368,19 +500,18 @@
         cost_estimate=pl.CostEstimate(
             flops=4 * rows * hidden * width, bytes_accessed=26 << 20, transcendentals=0
         ),
-        name=f"moe_step_{most_now}_{most_next}",
+        name=f"moe_step_{most}",
     )(table, live, saved, cot, weights, master, moment1, moment2)
 
 
 def exchanged(saved, cotangent, weights, counts, live_rows, next_map, master, moment1, moment2):
-    table, now, later = tables(counts, next_map, lax.axis_size("dev"))
+    devices = lax.axis_size("dev")
+    table, distinct = tables(counts, next_map, devices)
     args = (table, live_rows, saved[0], cotangent[0], weights[0], master, moment1, moment2)
-    few = GROUP - 1
-    fits = (now <= few) & (later <= few)
     outs = lax.cond(
-        fits,
-        functools.partial(fused, few, few, 0),
-        functools.partial(fused, GROUP, GROUP, 1),
+        distinct <= FEW,
+        functools.partial(fused, FEW, 0),
+        functools.partial(fused, devices // 2, 1),
         *args,
     )
     return (outs[0][None], outs[1], outs[2], outs[3], outs[4][None])
@@ -391,7 +522,7 @@
 
     def per_device(*args):
         share, width = args[6].shape[1:]
-        takes = devices % GROUP == 0 and GROUP >= MOST and share % 8 == 0
+        takes = devices == PLANES * GROUP and GROUP >= MOST and share % 8 == 0
         takes = takes and width % (CHUNKS * 128) == 0 and args[0].shape[1] % 256 == 0
         return (exchanged if takes else plain)(*args)
 

time: 166 us -> 164 us (0.988)
  between operations: 1.99 us -> 4.57 us
  other arithmetic: 3.29 us -> 1.22 us
  Pallas kernels: 147 us -> 145 us
    pallas_call x1, Pallas kernels: 147 us -> 145 us  [fused(): pl.pallas_call(functools.partial(kernel, most), out_shape=(jax.ShapeDtype...]
where the time goes in v2:
time: 164 us; the launch traced here: 163 us
  Pallas kernels  145 us (88%)
  local copies, waits for them, and re-layouts  12.6 us (8%)
  between operations  4.57 us (3%)
    pallas_call x1, Pallas kernels, fused(): pl.pallas_call(functools.partial(kernel, most), out_shape=(jax.ShapeDtype...  145 us
    unnamed x11, local copies, waits for them, and re-layouts  9.78 us

profile of v2, /device:TPU:0, one launch (start us, length us, event | category | flops | bytes accessed | tf_op | source)
XLA Modules:
  0.0 163.2 jit_solution(2562891219710220119)
XLA Ops:
  0.6 0.8 select_reduce_fusion.2
  1.4 0.1 convert_reduce_fusion.1
  1.5 0.7 eq.28
  2.2 0.1 convert_reduce_fusion
  2.4 0.1 select_reduce_fusion.1
  2.5 0.1 sub.17
  2.6 0.1 select_reduce_fusion
  2.7 0.1 reshape.45
  2.8 0.7 concatenate.3
  3.5 0.6 fusion.1
  5.4 0.6 fusion.2
  8.6 144.8 %conditional.1 = ((bf16[1024,768]{1,0:T(8,128)(2,1)S(1)}, f32[16,24,2048]{2,1,0:T(8,128)S(1)}, bf16[16,24,2048]{2,1,0:T(8,128)(2,1)}, bf16[16,24,2048]{2,1,0:T(8,128)(2,1)}, bf16[768,2048]{1,0:T(8,128)(2,1)})) conditional(s32[]{:T(128)} %convert_element_type.11, (bf16[1,1024,768]{2,1,0:T(8,128)(2,1)}, bf16[1,1024,2048]{2,1,0:T(8,128)(2,1)}, ...), branch_computations={%region_5.6_spmd, %region_6.7_spmd} | conditional | flops 6442450944 | bytes 27262984 | solution.py:511
  8.6 144.8 %moe_step_12.1 = (bf16[1024,768]{1,0:T(8,128)(2,1)S(1)}, f32[16,24,2048]{2,1,0:T(8,128)S(1)}, bf16[16,24,2048]{2,1,0:T(8,128)(2,1)}, bf16[16,24,2048]{2,1,0:T(8,128)(2,1)}, bf16[768,2048]{1,0:T(8,128)(2,1)}) custom-call(s32[144]{0:T(256)S(1)} %get-tuple-element.64.table, s32[1]{0:T(128)} %get-tuple-element.120.live, bf16[1024,768]{1,0:T(8,128)(2,1)} %bitcast.17, ...), custom_call_target="tpu_custom_call" | custom-call | flops 6442450944 | bytes 27262976 | tf_op jit(solution)/shard_map/cond/branch_1_fun/moe_step_12/pallas_call | solution.py:458
  153.4 1.1 copy.43
  154.5 0.0 copy-start.1
  154.5 1.7 %copy.44 = f32[16,24,2048]{2,1,0:T(8,128)} copy(f32[16,24,2048]{2,1,0:T(8,128)S(1)} %get-tuple-element.157) | data formatting | bytes 6291456
  156.2 0.9 copy-done.1
  157.1 0.0 copy-start.2
  157.1 1.1 copy.45
  158.2 0.8 copy-done.2
  159.1 0.0 copy-start
  159.1 1.1 copy.46
  160.2 1.3 copy-done
  161.5 1.7 %copy.47 = bf16[1,768,2048]{2,1,0:T(8,128)(2,1)} copy(bf16[1,768,2048]{2,1,0:T(8,128)(2,1)S(1)} %bitcast.10) | data formatting | bytes 6291456
  (3 shorter events, 0.0 us)
Async XLA Ops:
  154.5 2.5 %copy-start.1 = (bf16[16,24,2048]{2,1,0:T(8,128)(2,1)S(1)}, bf16[16,24,2048]{2,1,0:T(8,128)(2,1)}, u32[]{:S(2)}) copy-start(bf16[16,24,2048]{2,1,0:T(8,128)(2,1)} %get-tuple-element.158) | copy-start | bytes 4718596
  157.1 2.0 %copy-start.2 = (bf16[16,24,2048]{2,1,0:T(8,128)(2,1)S(1)}, bf16[16,24,2048]{2,1,0:T(8,128)(2,1)}, u32[]{:S(2)}) copy-start(bf16[16,24,2048]{2,1,0:T(8,128)(2,1)} %get-tuple-element.159) | copy-start | bytes 4718596
  159.1 2.5 %copy-start = (bf16[768,2048]{1,0:T(8,128)(2,1)S(1)}, bf16[768,2048]{1,0:T(8,128)(2,1)}, u32[]{:S(2)}) copy-start(bf16[768,2048]{1,0:T(8,128)(2,1)} %get-tuple-element.128) | copy-start | bytes 9437188

commit v3 on v2

--- a/solution.py
+++ b/solution.py
@@ -73,26 +73,68 @@
     )
 
 
-def tables(counts, next_map, devices):
-    experts = counts.shape[0]
-    slot = jnp.arange(devices, dtype=jnp.int32)
-    ids = jnp.arange(experts, dtype=jnp.int32)
-    upto = ids[None, :] <= ids[:, None]
-    bounds = jnp.sum(jnp.where(upto, counts[None, :], 0), axis=1)
-    holders = jnp.sum((bounds[None, :] <= slot[:, None]).astype(jnp.int32), axis=1)
+def plan(counts, next_map, table, distinct):
+    experts, devices = counts.shape[0], next_map.shape[0]
     half = devices // 2
-    upcoming = next_map.reshape(2, 1, half)
-    present = jnp.max((upcoming == ids[None, :, None]).astype(jnp.int32), axis=2)
-    place = jnp.sum(jnp.where(upto[None], present[:, None, :], 0), axis=2) - 1
-    at = (place[:, None, :] == jnp.arange(half, dtype=jnp.int32)[None, :, None]) & (
-        present[:, None, :] > 0
-    )
-    union = jnp.sum(jnp.where(at, ids[None, None, :], 0), axis=2)
-    table = jnp.concatenate(
-        [bounds, holders, next_map, place.reshape(-1), union.reshape(-1)]
-    ).astype(jnp.int32)
-    held = jnp.maximum(holders[half - 1] - holders[0], holders[devices - 1] - holders[half])
-    return table, jnp.maximum(held, jnp.maximum(place[0, -1], place[1, -1])) + 1
+    holder_at, next_at = experts, experts + devices
+    place_at = experts + 2 * devices
+    union_at = place_at + 2 * experts
+
+    def bound(e, total):
+        table[e] = total + counts[e]
+        return total + counts[e]
+
+    lax.fori_loop(0, experts, bound, jnp.int32(0))
+
+    def clear(i, _):
+        table[place_at + i] = 0
+        return _
+
+    lax.fori_loop(0, 2 * experts + devices, clear, jnp.int32(0))
+
+    def holder(s, e):
+        e = jnp.minimum(jnp.where(table[e] <= s, e + 1, e), experts - 1)
+        table[holder_at + s] = e
+        e_next = next_map[s]
+        table[next_at + s] = e_next
+        table[place_at + (s // half) * experts + e_next] = 1
+        return e
+
+    lax.fori_loop(0, devices, holder, jnp.int32(0))
+    most = jnp.maximum(
+        table[holder_at + half - 1] - table[holder_at],
+        table[holder_at + devices - 1] - table[holder_at + half],
+    )
+    most = most + 1
+    for h in range(2):
+
+        def rank(e, held, h=h):
+            here = table[place_at + h * experts + e]
+            table[place_at + h * experts + e] = held
+
+            @pl.when(here == 1)
+            def _():
+                table[union_at + h * half + held] = e
+
+            return held + here
+
+        most = jnp.maximum(most, lax.fori_loop(0, experts, rank, jnp.int32(0)))
+    distinct[0] = most
+
+
+def tables(counts, next_map):
+    experts, devices = counts.shape[0], next_map.shape[0]
+    scalars = pl.BlockSpec(memory_space=pltpu.SMEM)
+    return pl.pallas_call(
+        plan,
+        out_shape=(
+            jax.ShapeDtypeStruct((3 * experts + 3 * devices,), jnp.int32),
+            jax.ShapeDtypeStruct((1,), jnp.int32),
+        ),
+        in_specs=[scalars] * 2,
+        out_specs=(scalars,) * 2,
+        name="plan",
+    )(counts, next_map)
 
 
 def kernel(
@@ -216,7 +258,7 @@
 
     live_count = live[0]
     loads[0].wait()
-    step = 256
+    step = rows // 4
     for t in range(rows // step):
         index = lax.broadcasted_iota(jnp.int32, (step, hidden), 0) + t * step
         part = saved_v[t * step : (t + 1) * step, :].astype(f32)
@@ -225,8 +267,7 @@
 
     loads[1].wait()
 
-    @pl.loop(0, CHUNKS)
-    def _(c):
+    def multiply(c):
         grad_v[...] = jnp.dot(saved_t[...], cot_v[:, columns(c)], preferred_element_type=f32)
         for s in range(GROUP):
             parts = [
@@ -236,17 +277,12 @@
             xy_s[c, s] = jnp.concatenate(parts, axis=0).astype(bf16)
         send_xy(c)
 
-    loads[2].wait()
-
-    @pl.loop(0, rows // step)
-    def _(t):
-        at = pl.ds(pl.multiple_of(t * step, step), step)
-        index = lax.broadcasted_iota(jnp.int32, (step, hidden), 0) + t * step
+    def turn_back(t):
+        few = rows // CHUNKS
+        at = pl.ds(pl.multiple_of(t * few, few), few)
+        index = lax.broadcasted_iota(jnp.int32, (few, hidden), 0) + t * few
         out = contract_cols(cot_v[at, :], weights_v[...])
         ig_v[at, :] = jnp.where(index < live_count, out, 0.0).astype(bf16)
-
-    ig_store = pltpu.make_async_copy(ig_v, ig_out, load_sem.at[6])
-    ig_store.start()
 
     holder_at, next_at = experts, experts + devices
     place_at = experts + 2 * devices
@@ -284,37 +320,55 @@
         across_inner(c).start()
         across_outer(c).start()
 
-    @pl.loop(0, CHUNKS + 1)
+    def reduce(c):
+        arrived_xy(c)
+        for p in range(planes):
+            total = jnp.zeros((share, wide), f32)
+            for s in range(GROUP):
+                now = plane * GROUP + s
+                if s:
+                    same = table[holder_at + now] == table[holder_at + now - 1]
+                    total = total * jnp.where(same, 1.0, 0.0)
+                total = total + xy_r[c, s].astype(f32)[p * share : (p + 1) * share, :]
+                sums[p, s] = total.astype(bf16)
+        for k in range(GROUP):
+            e = jnp.minimum(held_own[0] + k, experts - 1)
+            last = jnp.clip(table[e] - 1 - plane * GROUP, 0, GROUP - 1)
+            half_s[c, 0, k] = sums[far_inner, last]
+            half_s[c, 1, k] = sums[far_outer, last]
+            mate_s[c, k] = sums[mate, last]
+            own_v[c, k] = sums[plane, last]
+
+        @pl.when(jnp.logical_not(is_inner))
+        def _():
+            half_to_mate(c).start()
+
+        to_mate(c).start()
+
+    for c in range(2):
+        multiply(c)
+    loads[2].wait()
+
+    @pl.loop(2, CHUNKS + 3)
     def _(c):
         @pl.when(c < CHUNKS)
         def _():
-            arrived_xy(c)
-            for p in range(planes):
-                total = jnp.zeros((share, wide), f32)
-                for s in range(GROUP):
-                    now = plane * GROUP + s
-                    if s:
-                        same = table[holder_at + now] == table[holder_at + now - 1]
-                        total = total * jnp.where(same, 1.0, 0.0)
-                    total = total + xy_r[c, s].astype(f32)[p * share : (p + 1) * share, :]
-                    sums[p, s] = total.astype(bf16)
-            for k in range(GROUP):
-                e = jnp.minimum(held_own[0] + k, experts - 1)
-                last = jnp.clip(table[e] - 1 - plane * GROUP, 0, GROUP - 1)
-                half_s[c, 0, k] = sums[far_inner, last]
-                half_s[c, 1, k] = sums[far_outer, last]
-                mate_s[c, k] = sums[mate, last]
-                own_v[c, k] = sums[plane, last]
-
-            @pl.when(jnp.logical_not(is_inner))
-            def _():
-                half_to_mate(c).start()
-
-            to_mate(c).start()
-
-        @pl.when((c > 0) & is_inner)
-        def _():
-            combine(c - 1)
+            multiply(c)
+
+        @pl.when(c < CHUNKS + 2)
+        def _():
+            reduce(c - 2)
+
+        @pl.when((c > 2) & is_inner)
+        def _():
+            combine(c - 3)
+
+        @pl.when(c < CHUNKS + 2)
+        def _():
+            turn_back(c - 2)
+
+    ig_store = pltpu.make_async_copy(ig_v, ig_out, load_sem.at[6])
+    ig_store.start()
 
     for load in loads[3:]:
         load.wait()
@@ -506,10 +560,10 @@
 
 def exchanged(saved, cotangent, weights, counts, live_rows, next_map, master, moment1, moment2):
     devices = lax.axis_size("dev")
-    table, distinct = tables(counts, next_map, devices)
+    table, distinct = tables(counts, next_map)
     args = (table, live_rows, saved[0], cotangent[0], weights[0], master, moment1, moment2)
     outs = lax.cond(
-        distinct <= FEW,
+        distinct[0] <= FEW,
         functools.partial(fused, FEW, 0),
         functools.partial(fused, devices // 2, 1),
         *args,
@@ -523,7 +577,7 @@
     def per_device(*args):
         share, width = args[6].shape[1:]
         takes = devices == PLANES * GROUP and GROUP >= MOST and share % 8 == 0
-        takes = takes and width % (CHUNKS * 128) == 0 and args[0].shape[1] % 256 == 0
+        takes = takes and width % (CHUNKS * 128) == 0 and args[0].shape[1] % (CHUNKS * 16) == 0
         return (exchanged if takes else plain)(*args)
 
     placed = (

time: 164 us -> 160 us (0.976)
  Pallas kernels: 145 us -> 149 us
  between operations: 4.57 us -> 1.3 us
  local copies, waits for them, and re-layouts: 12.6 us -> 9.78 us
    pallas_call x0 -> x1, Pallas kernels: none -> 2.52 us  [tables(): pl.pallas_call(plan, out_shape=(jax.ShapeDtypeStruct((3 * experts + 3 * d...]
where the time goes in v3:
time: 160 us
  Pallas kernels  149 us (93%)
  local copies, waits for them, and re-layouts  9.78 us (6%)
    pallas_call x1, Pallas kernels, fused(): pl.pallas_call(functools.partial(kernel, most), out_shape=(jax.ShapeDtype...  146 us
    unnamed x11, local copies, waits for them, and re-layouts  9.78 us

profile of v3, /device:TPU:0, one launch (start us, length us, event | category | flops | bytes accessed | tf_op | source)
XLA Modules:
  0.0 160.0 jit_solution(10735678985130742870)
XLA Ops:
  0.6 2.5 %plan.1 = (s32[144]{0:T(256)S(1)}, s32[1]{0:T(128)}) custom-call(s32[16]{0:T(128)} %counts.1, s32[32]{0:T(128)} %next_map.1), custom_call_target="tpu_custom_call" | custom-call | tf_op jit(solution)/shard_map/plan/pallas_call | solution.py:128
  3.8 146.4 %conditional.1 = ((bf16[1024,768]{1,0:T(8,128)(2,1)S(1)}, f32[16,24,2048]{2,1,0:T(8,128)S(1)}, bf16[16,24,2048]{2,1,0:T(8,128)(2,1)}, bf16[16,24,2048]{2,1,0:T(8,128)(2,1)}, bf16[768,2048]{1,0:T(8,128)(2,1)})) conditional(s32[]{:T(128)} %bitcast, (s32[144]{0:T(256)S(1)}, s32[1]{0:T(128)}, bf16[1024,768]{1,0:T(8,128)(2,1)}, ...), branch_computations={%region_0.0_spmd, %region_1.0_spmd} | conditional | flops 6442450944 | bytes 27262984 | solution.py:565
  3.8 146.4 %moe_step_12.1 = (bf16[1024,768]{1,0:T(8,128)(2,1)S(1)}, f32[16,24,2048]{2,1,0:T(8,128)S(1)}, bf16[16,24,2048]{2,1,0:T(8,128)(2,1)}, bf16[16,24,2048]{2,1,0:T(8,128)(2,1)}, bf16[768,2048]{1,0:T(8,128)(2,1)}) custom-call(s32[144]{0:T(256)S(1)} %get-tuple-element.58.table, s32[1]{0:T(128)} %get-tuple-element.59.live, ...), custom_call_target="tpu_custom_call" | custom-call | flops 6442450944 | bytes 27262976 | tf_op jit(solution)/shard_map/cond/branch_1_fun/moe_step_12/pallas_call | solution.py:512
  150.2 1.1 copy.29
  151.4 0.0 copy-start.1
  151.4 1.7 %copy.30 = f32[16,24,2048]{2,1,0:T(8,128)} copy(f32[16,24,2048]{2,1,0:T(8,128)S(1)} %get-tuple-element.121) | data formatting | bytes 6291456
  153.0 0.9 copy-done.1
  153.9 0.0 copy-start.2
  153.9 1.1 copy.31
  155.0 0.8 copy-done.2
  155.9 0.0 copy-start
  155.9 1.1 copy.32
  157.0 1.3 copy-done
  158.3 1.7 %copy.33 = bf16[1,768,2048]{2,1,0:T(8,128)(2,1)} copy(bf16[1,768,2048]{2,1,0:T(8,128)(2,1)S(1)} %bitcast.6) | data formatting | bytes 6291456
Async XLA Ops:
  151.4 2.5 %copy-start.1 = (bf16[16,24,2048]{2,1,0:T(8,128)(2,1)S(1)}, bf16[16,24,2048]{2,1,0:T(8,128)(2,1)}, u32[]{:S(2)}) copy-start(bf16[16,24,2048]{2,1,0:T(8,128)(2,1)} %get-tuple-element.122) | copy-start | bytes 4718596
  153.9 2.0 %copy-start.2 = (bf16[16,24,2048]{2,1,0:T(8,128)(2,1)S(1)}, bf16[16,24,2048]{2,1,0:T(8,128)(2,1)}, u32[]{:S(2)}) copy-start(bf16[16,24,2048]{2,1,0:T(8,128)(2,1)} %get-tuple-element.123) | copy-start | bytes 4718596
  155.9 2.5 %copy-start = (bf16[768,2048]{1,0:T(8,128)(2,1)S(1)}, bf16[768,2048]{1,0:T(8,128)(2,1)}, u32[]{:S(2)}) copy-start(bf16[768,2048]{1,0:T(8,128)(2,1)} %get-tuple-element.98) | copy-start | bytes 9437188

commit v4 on v3

--- a/solution.py
+++ b/solution.py
@@ -15,7 +15,7 @@
 BIAS_TWO = 1.0 - 0.95**20
 EPSILON = 1e-08
 GROUP = 8
-CHUNKS = 8
+CHUNKS = 16
 PLANES = 4
 MOST = 8
 FEW = 12
@@ -141,15 +141,16 @@
     most,
     table, live, saved, cot, weights, master, moment1, moment2,
     ig_out, master_out, moment1_out, moment2_out, next_out,
-    saved_v, saved_t, cot_v, weights_v, master_v, moment1_v, moment2_v, ig_v, next_v,
+    saved_v, saved_t, cot_v, weights_v, master_v, moment1_v, moment2_v,
     grad_v, sums, fresh, own_v, half_v, mate_v, cross_v, union_v, gather_v,
     xy_s, xy_r, half_s, half_r, mate_s, mate_r, cross_s, cross_r,
-    union_s, union_r, back_s, back_r, pass_s, pass_r, nxy_s, nxy_r,
-    load_sem, s1, r1, s2, r2, s4, r4,
+    union_s, union_r, back_s, back_r, pass_s, pass_r, nxy_r,
+    load_sem, s1, r1, s2, r2, s4, r4, s5,
 ):
     me = lax.axis_index("dev")
     plane, spot = me // GROUP, lax.rem(me, GROUP)
     planes, devices = PLANES, PLANES * GROUP
+    ig_v, next_v, nxy_s = saved_v, weights_v, xy_s
     side = plane // 2
     inner = 1 + side
     is_inner = plane == inner
@@ -263,7 +264,7 @@
         index = lax.broadcasted_iota(jnp.int32, (step, hidden), 0) + t * step
         part = saved_v[t * step : (t + 1) * step, :].astype(f32)
         part = jnp.where(index < live_count, part, 0.0)
-        saved_t[:, t * step : (t + 1) * step] = part.T.astype(bf16)
+        saved_t[:, t * step : (t + 1) * step] = part.astype(bf16).T
 
     loads[1].wait()
 
@@ -373,6 +374,10 @@
     for load in loads[3:]:
         load.wait()
 
+    @pl.loop(0, CHUNKS)
+    def _(c):
+        sent_xy(c)
+
     def update(c):
         to_mate(c).wait_recv()
         across_inner(c).wait_recv()
@@ -462,6 +467,10 @@
     for store in stores:
         store.start()
 
+    def store_next(c):
+        cols = columns(c)
+        return pltpu.make_async_copy(next_v.at[:, cols], next_out.at[:, cols], s5.at[c])
+
     @pl.loop(0, CHUNKS)
     def _(c):
         arrived_nxy(c)
@@ -472,17 +481,15 @@
                 ]
                 at = (p * GROUP + s) * share
                 next_v[at : at + 2 * share, columns(c)] = jnp.concatenate(pair, axis=0).astype(bf16)
-
-    store = pltpu.make_async_copy(next_v, next_out, load_sem.at[10])
-    store.start()
+        store_next(c).start()
 
     @pl.loop(0, CHUNKS)
     def _(c):
-        sent_xy(c)
         to_mate(c).wait_send()
         union_to_far(c, parity).wait_send()
         back_to_mate(c).wait_send()
         sent_nxy(c)
+        store_next(c).wait()
 
         @pl.when(is_inner)
         def _():
@@ -494,7 +501,7 @@
         def _():
             half_to_mate(c).wait_send()
 
-    for done in [ig_store] + stores + [store]:
+    for done in [ig_store] + stores:
         done.wait()
 
 
@@ -528,8 +535,6 @@
             vmem(master.shape, f32),
             vmem(moment1.shape, bf16),
             vmem(moment2.shape, bf16),
-            vmem((rows, hidden), bf16),
-            vmem((hidden, width), bf16),
             vmem((hidden, wide), f32),
             blocks(PLANES, GROUP),
             blocks(CHUNKS, experts),
@@ -542,14 +547,15 @@
             blocks(CHUNKS, most), blocks(CHUNKS, 2, most),
             blocks(CHUNKS, GROUP), blocks(CHUNKS, GROUP),
             blocks(CHUNKS, 2, GROUP), blocks(CHUNKS, 2, GROUP),
-            across, across,
+            across,
             dma((11,)),
             dma((CHUNKS, GROUP)), dma((CHUNKS, GROUP)),
             dma((CHUNKS, 7)), dma((CHUNKS, 7)),
             dma((CHUNKS, GROUP)), dma((CHUNKS, GROUP)),
+            dma((CHUNKS,)),
         ],
         compiler_params=pltpu.CompilerParams(
-            collective_id=number, has_side_effects=True, vmem_limit_bytes=58 * 1024 * 1024
+            collective_id=number, has_side_effects=True, vmem_limit_bytes=50 * 1024 * 1024
         ),
         cost_estimate=pl.CostEstimate(
             flops=4 * rows * hidden * width, bytes_accessed=26 << 20, transcendentals=0

time: 160 us -> 152 us (0.950)
  Pallas kernels: 149 us -> 144 us
  local copies, waits for them, and re-layouts: 9.78 us -> 6.76 us
    pallas_call x1, Pallas kernels: 146 us -> 141 us  [fused(): pl.pallas_call(functools.partial(kernel, most), out_shape=(jax.ShapeDtype...]
    unnamed x11 -> x5, local copies, waits for them, and re-layouts: 9.78 us -> 6.76 us
where the time goes in v4:
time: 152 us
  Pallas kernels  144 us (95%)
  local copies, waits for them, and re-layouts  6.76 us (4%)
    pallas_call x1, Pallas kernels, fused(): pl.pallas_call(functools.partial(kernel, most), out_shape=(jax.ShapeDtype...  141 us
    unnamed x5, local copies, waits for them, and re-layouts  6.76 us

profile of v4, /device:TPU:0, one launch (start us, length us, event | category | flops | bytes accessed | tf_op | source)
XLA Modules:
  0.0 151.9 jit_solution(7294157100056776483)
XLA Ops:
  0.6 2.5 %plan.1 = (s32[144]{0:T(256)S(1)}, s32[1]{0:T(128)}) custom-call(s32[16]{0:T(128)} %counts.1, s32[32]{0:T(128)} %next_map.1), custom_call_target="tpu_custom_call" | custom-call | tf_op jit(solution)/shard_map/plan/pallas_call | solution.py:128
  3.8 141.3 %conditional.1 = ((bf16[1024,768]{1,0:T(8,128)(2,1)S(1)}, f32[16,24,2048]{2,1,0:T(8,128)S(1)}, bf16[16,24,2048]{2,1,0:T(8,128)(2,1)S(1)}, bf16[16,24,2048]{2,1,0:T(8,128)(2,1)S(1)}, bf16[768,2048]{1,0:T(8,128)(2,1)S(1)})) conditional(s32[]{:T(128)} %bitcast, (s32[144]{0:T(256)S(1)}, s32[1]{0:T(128)}, bf16[1024,768]{1,0:T(8,128)(2,1)}, ...), branch_computations={%region_0.0_spmd, %region_1.0_spmd} | conditional | flops 6442450944 | bytes 27262984 | solution.py:571
  3.8 141.3 %moe_step_12.1 = (bf16[1024,768]{1,0:T(8,128)(2,1)S(1)}, f32[16,24,2048]{2,1,0:T(8,128)S(1)}, bf16[16,24,2048]{2,1,0:T(8,128)(2,1)S(1)}, bf16[16,24,2048]{2,1,0:T(8,128)(2,1)S(1)}, bf16[768,2048]{1,0:T(8,128)(2,1)S(1)}) custom-call(s32[144]{0:T(256)S(1)} %get-tuple-element.58.table, s32[1]{0:T(128)} %get-tuple-element.59.live, ...), custom_call_target="tpu_custom_call" | custom-call | flops 6442450944 | bytes 27262976 | tf_op jit(solution)/shard_map/cond/branch_1_fun/moe_step_12/pallas_call | solution.py:519
  145.1 1.1 copy.29
  146.3 1.7 %copy.30 = f32[16,24,2048]{2,1,0:T(8,128)} copy(f32[16,24,2048]{2,1,0:T(8,128)S(1)} %get-tuple-element.121) | data formatting | bytes 6291456
  147.9 1.1 copy.31
  149.1 1.1 copy.32
  150.2 1.7 %copy.33 = bf16[1,768,2048]{2,1,0:T(8,128)(2,1)} copy(bf16[1,768,2048]{2,1,0:T(8,128)(2,1)S(1)} %bitcast.6) | data formatting | bytes 6291456

commit v5 on v4

--- a/solution.py
+++ b/solution.py
@@ -18,7 +18,7 @@
 CHUNKS = 16
 PLANES = 4
 MOST = 8
-FEW = 12
+WIDTHS = (11, 13)
 MESH = pl.DeviceIdType.MESH
 
 
@@ -344,7 +344,9 @@
         def _():
             half_to_mate(c).start()
 
-        to_mate(c).start()
+        @pl.when(is_inner)
+        def _():
+            to_mate(c).start()
 
     for c in range(2):
         multiply(c)
@@ -367,6 +369,12 @@
         @pl.when(c < CHUNKS + 2)
         def _():
             turn_back(c - 2)
+
+    @pl.when(jnp.logical_not(is_inner))
+    def _():
+        @pl.loop(0, CHUNKS)
+        def _(c):
+            to_mate(c).start()
 
     ig_store = pltpu.make_async_copy(ig_v, ig_out, load_sem.at[6])
     ig_store.start()
@@ -568,11 +576,10 @@
     devices = lax.axis_size("dev")
     table, distinct = tables(counts, next_map)
     args = (table, live_rows, saved[0], cotangent[0], weights[0], master, moment1, moment2)
-    outs = lax.cond(
-        distinct[0] <= FEW,
-        functools.partial(fused, FEW, 0),
-        functools.partial(fused, devices // 2, 1),
-        *args,
+    widths = WIDTHS + (devices // 2,)
+    which = sum((distinct[0] > width).astype(jnp.int32) for width in WIDTHS)
+    outs = lax.switch(
+        which, [functools.partial(fused, width, i) for i, width in enumerate(widths)], *args
     )
     return (outs[0][None], outs[1], outs[2], outs[3], outs[4][None])
 

time: 152 us -> 144 us (0.947)
  Pallas kernels: 144 us -> 135 us
    pallas_call x1, Pallas kernels: 141 us -> 133 us  [fused(): pl.pallas_call(functools.partial(kernel, most), out_shape=(jax.ShapeDtype...]
where the time goes in v5:
time: 144 us
  Pallas kernels  135 us (94%)
  local copies, waits for them, and re-layouts  6.76 us (5%)
  between operations  1.95 us (1%)
    pallas_call x1, Pallas kernels, fused(): pl.pallas_call(functools.partial(kernel, most), out_shape=(jax.ShapeDtype...  133 us
    unnamed x5, local copies, waits for them, and re-layouts  6.76 us

profile of v5, /device:TPU:0, one launch (start us, length us, event | category | flops | bytes accessed | tf_op | source)
XLA Modules:
  0.0 144.3 jit_solution(3467748238716587173)
XLA Ops:
  0.6 2.5 %plan.1 = (s32[144]{0:T(256)S(1)}, s32[1]{0:T(128)}) custom-call(s32[16]{0:T(128)} %counts.1, s32[32]{0:T(128)} %next_map.1), custom_call_target="tpu_custom_call" | custom-call | tf_op jit(solution)/shard_map/plan/pallas_call | solution.py:128
  4.5 133.1 %conditional.1 = ((bf16[1024,768]{1,0:T(8,128)(2,1)S(1)}, f32[16,24,2048]{2,1,0:T(8,128)S(1)}, bf16[16,24,2048]{2,1,0:T(8,128)(2,1)S(1)}, bf16[16,24,2048]{2,1,0:T(8,128)(2,1)S(1)}, bf16[768,2048]{1,0:T(8,128)(2,1)S(1)})) conditional(s32[]{:T(128)} %bitcast, (s32[144]{0:T(256)S(1)}, s32[1]{0:T(128)}, bf16[1024,768]{1,0:T(8,128)(2,1)}, ...), branch_computations={%region_0.0_spmd, %region_1.0_spmd, %region_2.0_spmd} | conditional | flops 6442450944 | bytes 27262984 | solution.py:581
  4.5 132.8 %moe_step_11.1 = (bf16[1024,768]{1,0:T(8,128)(2,1)S(1)}, f32[16,24,2048]{2,1,0:T(8,128)S(1)}, bf16[16,24,2048]{2,1,0:T(8,128)(2,1)S(1)}, bf16[16,24,2048]{2,1,0:T(8,128)(2,1)S(1)}, bf16[768,2048]{1,0:T(8,128)(2,1)S(1)}) custom-call(s32[144]{0:T(256)S(1)} %get-tuple-element.71.table, s32[1]{0:T(128)} %get-tuple-element.72.live, ...), custom_call_target="tpu_custom_call" | custom-call | flops 6442450944 | bytes 27262976 | tf_op jit(solution)/shard_map/cond/branch_0_fun/moe_step_11/pallas_call | solution.py:527
  137.5 1.1 copy.34
  138.7 1.7 %copy.35 = f32[16,24,2048]{2,1,0:T(8,128)} copy(f32[16,24,2048]{2,1,0:T(8,128)S(1)} %get-tuple-element.161) | data formatting | bytes 6291456
  140.3 1.1 copy.36
  141.5 1.1 copy.37
  142.6 1.7 %copy.38 = bf16[1,768,2048]{2,1,0:T(8,128)(2,1)} copy(bf16[1,768,2048]{2,1,0:T(8,128)(2,1)S(1)} %bitcast.6) | data formatting | bytes 6291456
